TPU v7x, 32 devices: a whole 2x2x4 slice. The times are simulated.
32 devices in a mesh: src: 8 (over z, y), tgt: 4 (over x, core).
Axes of the slice: x: 2, y: 2, z: 4, core: 2. Of those that a mesh axis runs over, the one named last changes fastest.
Arguments:
- particle_position: float32 [3, 12288], P(None, ('src', 'tgt')), may hold values from 0 to 1, as said below
- particle_strength: float32 [3, 12288], P(None, ('src', 'tgt')), may hold values from -6 to 6
- core_radius: float32 [1, 12288], P(None, ('src', 'tgt')), may hold values from 0.05 to 0.12
- boundary_points: float32 [3, 8, 256], P(None, None, 'tgt'), may hold values from 0 to 1, as said below
- vorticity: float32 [8, 3, 256, 128], P('src', None, 'tgt'), may hold values from -6 to 6
- swirl: float32 [8, 256, 128], P('src', 'tgt'), may hold values from -0.5 to 0.5
- diffusivity: float32 [8, 256, 128], P('src', 'tgt'), may hold values from 0.05 to 0.2
- intersection_source: int32 [8, 4, 9], P('src', 'tgt'), may hold values from 0 to 191
- intersection_target: int32 [8, 4, 9], P('src', 'tgt'), may hold values from -1 to 35, as said below
Outputs:
- wall_velocity: float32 [3, 8, 256], P(None, 'src', 'tgt')
- grid_vorticity: float32 [8, 3, 256, 128], P('src', None, 'tgt')
- new_strength: float32 [3, 12288], P(None, ('src', 'tgt'))
Inputs may be any that keep to these rules, and one draw needn't show every extreme that they name: `particle_position`: every coordinate of every particle lies in [0, 1). `boundary_points`: point (z, a) has its first two coordinates in [0, 1) and its third in [z / 8, (z + 1) / 8). `intersection_target`: an entry of list (s, t) is -1 or owner * 9 + block, naming particle block block of device (s, owner). Live entries stand before the -1 entries. Over all lists of one src index each particle block of each device is named at most once. No list names one owner in more than 4 live entries, and some list names some owner in exactly 4; some list has 9 live entries.
All inputs are finite; a program needn't handle non-finite values.
Results may differ from a plain program's by a relative error of at most 0.0003.
Values sent between devices are 32-bit elements; how exact they have to be, the bound alone decides.
No kernel may reach another device: no remote copies, remote signals or barrier semaphores. Data moves between devices by JAX's collectives and lax.ppermute only.
A program may use at most 64 MiB of HBM per device.

v0:
```python
import functools
import math

import jax
import jax.numpy as jnp
from jax import lax
from jax.experimental import pallas as pl
from jax.experimental.pallas import tpu as pltpu
from jax.sharding import PartitionSpec as P

SUBSTEPS = 3
LANES = 128
ROWS = 8
TOGETHER = 2
TERMS = 48
UNROLLED = 4
swirl_gain = 0.2
f32 = jnp.float32
bf16 = jnp.bfloat16


def vmem():
    return pl.BlockSpec(memory_space=pltpu.VMEM)


def smem():
    return pl.BlockSpec(memory_space=pltpu.SMEM)


def hbm():
    return pl.BlockSpec(memory_space=pltpu.HBM)


def stay(*arrays):
    return [pltpu.with_memory_space_constraint(a, pltpu.HBM) for a in arrays]


def shape(*dims):
    return jax.ShapeDtypeStruct(dims, f32)


def limit(megabytes):
    return pltpu.CompilerParams(vmem_limit_bytes=megabytes << 20)


def cost(flops, size):
    return pl.CostEstimate(flops=flops, bytes_accessed=size, transcendentals=0)


def divisor(number, most):
    return max(c for c in range(1, min(number, most) + 1) if number % c == 0)


def power_of_two(number):
    return number & (number - 1) == 0


def partner(index, step, count):
    return index ^ step if power_of_two(count) else (index + step) % count


def source_of(index, step, count):
    return index ^ step if power_of_two(count) else (index - step) % count


def line_order(outer):
    return [0, *range(outer // 2, outer), *range(1, outer // 2)]


def tgt_order(ways):
    return [0, *range(ways // 2, ways), *range(1, ways // 2)]


def turn(step, ways):
    return {1: 3, 3: 1}.get(step % ways, step % ways)


def particles_kernel(inner, outer, *refs):
    given, messages = refs[:9], refs[9 : 9 + outer]
    own, lists, held, sems = refs[9 + outer], refs[10 + outer : 12 + outer], refs[12 + outer : -1], refs[-1]
    vort, swirl, diff = given[4:7]
    targets = (*held, *[own.at[c] for c in range(5)], *lists)
    sources = (*given[0:4], *[vort.at[0, m] for m in range(3)], swirl.at[0], diff.at[0], *given[7:9])
    copies = [
        pltpu.make_async_copy(a, b, sems.at[i]) for i, (a, b) in enumerate(zip(sources, targets))
    ]
    for copy in copies:
        copy.start()
    for copy in copies[0:4]:
        copy.wait()
    pos, strength, radius, points = held
    tiles = pos.shape[1] // LANES
    angles = points.shape[2]
    src = lax.axis_index("src")
    core = radius[...] * radius[...]
    parts = [slice(k * LANES, (k + 1) * LANES) for k in range(tiles)]
    bare = [
        jnp.concatenate(
            [pos[:, part], strength[:, part], core[:, part], jnp.zeros((1, LANES), f32)], axis=0
        )
        for part in parts
    ]
    last = lax.broadcasted_iota(jnp.int32, (ROWS, LANES), 0) == ROWS - 1
    for step, message in zip(line_order(outer), messages):
        there = partner(src // inner, step, outer) * inner
        planes = (there + src % inner, there + inner - 1 - src % inner)
        for k in range(tiles):
            if k < 3:
                both = [points[k, pl.ds(plane, 1), :] for plane in planes]
                both.append(jnp.zeros((1, LANES - 2 * angles), f32))
                both = [p for p in both if p.shape[1]]
                message[k] = jnp.where(last, jnp.concatenate(both, axis=1), bare[k])
            else:
                message[k] = bare[k]
    for copy in copies[4:]:
        copy.wait()


def edges_kernel(own, own_source, own_target, message):
    angles = own.shape[1]
    blocks = own_source.shape[2]
    total = angles * lax.axis_size("tgt")
    half = ROWS // 2
    for c in range(5):
        message[c, :, 0:angles] = jnp.transpose(own[c])[0:ROWS, :]
        message[c, :, angles:LANES] = jnp.zeros((ROWS, LANES - angles), f32)
        message[6 + c, 0:half, :] = own[c, 0:half]
        message[6 + c, half:ROWS, :] = own[c, angles - half : angles]
    message[5] = jnp.full((ROWS, LANES), -1.0, f32)
    q = own_source[0]
    row = (q // angles) * total + lax.axis_index("tgt") * angles + q % angles
    message[5, 0:1, 0:blocks] = row.astype(f32)
    message[5, 1:2, 0:blocks] = own_target[0].astype(f32)


def inner_step(field, local_swirl, local_diff, speed, first):
    total = field[0].shape[1]
    transport = 0.5 * (local_swirl + swirl_gain * field[2])
    renewed = []
    for m in range(3):
        center = field[m]
        eastern = pltpu.roll(center, total - 1, 1)
        western = pltpu.roll(center, 1, 1)
        outward = pltpu.roll(center, ROWS - 1, 0)
        inward = jnp.where(first, speed[m], pltpu.roll(center, 1, 0))
        renewed.append(
            center
            + local_diff * (eastern + western + outward + inward - 4.0 * center)
            - transport * (eastern - western)
        )
    return renewed


def still_kernel(ways, *refs):
    messages = refs[:ways]
    own, lists, after, grid, picks, placed, source, sem = refs[ways:]
    copy = pltpu.make_async_copy(lists, source, sem)
    copy.start()
    angles = own.shape[1]
    height = angles + ROWS
    blocks = lists.shape[2]
    me = lax.axis_index("tgt")
    for step, message in zip(tgt_order(ways), messages):
        placed[source_of(me, step, ways)] = message[6:11]

    upper = lax.broadcasted_iota(jnp.int32, (ROWS, LANES), 0) < ROWS // 2
    east = lax.rem(me + 1, ways)
    west = lax.rem(me + ways - 1, ways)
    cells = [
        jnp.concatenate(
            [own[c], jnp.where(upper, placed[east, c], placed[west, c])], axis=0
        )
        for c in range(5)
    ]
    field, local_swirl, local_diff = cells[0:3], cells[3], cells[4]
    lane = lax.broadcasted_iota(jnp.int32, (height, LANES), 1)
    for counter in range(SUBSTEPS):
        transport = 0.5 * (local_swirl + swirl_gain * field[2])
        renewed = []
        for m in range(3):
            center = field[m]
            eastern = pltpu.roll(center, height - 1, 0)
            western = pltpu.roll(center, 1, 0)
            outward = jnp.where(lane == LANES - 1, 0.0, pltpu.roll(center, LANES - 1, 1))
            inward = jnp.where(lane == 0, 0.0, pltpu.roll(center, 1, 1))
            renewed.append(
                center
                + local_diff * (eastern + western + outward + inward - 4.0 * center)
                - transport * (eastern - western)
            )
        field = renewed
    for m in range(3):
        grid[m] = field[m][0:angles]
    picks[...] = jnp.zeros(picks.shape, f32)
    copy.wait()
    for i in range(blocks):
        q = source[0, 0, i]
        picks[i : i + 1, :] = grid[q // angles, pl.ds(q % angles, 1), :]


def three_parts(value):
    high = value.astype(bf16).astype(f32)
    rest = value - high
    middle = rest.astype(bf16).astype(f32)
    return high, middle, rest - middle


def middle_of(outer, inner):
    here = (lax.axis_index("src") // inner).astype(f32)
    return 0.5, 0.5, (here + 0.5) * (1.0 / outer)


def point_terms(message, lane, angles, middle):
    x, y, z = [message[m, 7:8, lane : lane + angles] - middle[m] for m in range(3)]
    nothing = jnp.zeros((3, angles), f32)
    vector = jnp.concatenate(
        [-2.0 * x, -2.0 * y, -2.0 * z, jnp.ones_like(x), x * x + y * y + z * z, nothing], axis=0
    )
    high, middling, low = three_parts(vector)
    terms = jnp.transpose(jnp.concatenate([high, middling, low, high, middling, high], axis=0))
    return jnp.concatenate([x, y, z, nothing, nothing[0:2]], axis=0), terms.astype(bf16)


def tile_terms(message, middle, moments, others):
    one = jnp.ones((1, LANES), f32)
    nothing = jnp.zeros((3, LANES), f32)
    for k in range(message.shape[0]):
        px, py, pz = [message[k, r : r + 1, :] - middle[r] for r in range(3)]
        sx, sy, sz, cc = [message[k, r : r + 1, :] for r in range(3, 7)]
        moments[k] = jnp.concatenate(
            [sx, sy, sz, sy * pz - sz * py, sz * px - sx * pz, sx * py - sy * px, nothing[0:2]],
            axis=0,
        )
        vector = jnp.concatenate(
            [px, py, pz, px * px + py * py + (pz * pz + cc), one, nothing], axis=0
        )
        high, middling, low = three_parts(vector)
        others[:, k * LANES : (k + 1) * LANES] = jnp.concatenate(
            [high, high, high, middling, middling, low], axis=0
        ).astype(bf16)


def quarter(terms, blocks):
    tall = terms.shape[0]
    diagonal = lax.broadcasted_iota(jnp.int32, (ROWS, LANES), 1) - lax.broadcasted_iota(
        jnp.int32, (ROWS, LANES), 0
    )
    distances = [
        jnp.dot(terms, others[...], preferred_element_type=f32) for moments, others in blocks
    ]
    rows = [jnp.zeros((ROWS, LANES), f32)] * 6
    for start in range(0, tall // ROWS, TOGETHER):
        held = [jnp.zeros((ROWS, LANES), f32)] * (6 * TOGETHER)
        for distance, (moments, others) in zip(distances, blocks):
            for k in range(moments.shape[0]):
                summed = [moments[k, r : r + 1, :] for r in range(6)]
                for i in range(TOGETHER):
                    low = (start + i) * ROWS
                    inverse = lax.rsqrt(distance[low : low + ROWS, k * LANES : (k + 1) * LANES])
                    weight = inverse * inverse * inverse
                    for r in range(6):
                        held[6 * i + r] += weight * summed[r]
        for i in range(TOGETHER):
            mask = diagonal == (start + i) * ROWS
            for r in range(6):
                value = jnp.sum(held[6 * i + r], axis=1, keepdims=True)
                rows[r] = rows[r] + jnp.where(mask, value, 0.0)
    return rows


def repeat(count, body, carried):
    if count <= UNROLLED:
        for i in range(count):
            carried = body(i, carried)
        return carried
    return lax.fori_loop(0, count, body, carried)


def quarter_speed(scale, along, terms, blocks):
    if isinstance(blocks, list):
        rows = quarter(terms, blocks)
    else:
        moments, others = blocks
        count = others.shape[0]
        if count <= UNROLLED:
            rows = quarter(terms, [(moments.at[i], others.at[i]) for i in range(count)])
        else:

            def add(i, rows):
                more = quarter(terms, [(moments.at[i], others.at[i])])
                return tuple(a + b for a, b in zip(rows, more))

            rows = lax.fori_loop(0, count, add, (jnp.zeros((ROWS, LANES), f32),) * 6)
    angles = terms.shape[0]
    ax, ay, az, bx, by, bz = [jnp.sum(r, axis=0, keepdims=True) for r in rows]
    tx, ty, tz = [
        jnp.concatenate([along[m : m + 1, :], jnp.zeros((1, LANES - angles), f32)], axis=1)
        for m in range(3)
    ]
    return jnp.concatenate(
        [
            scale * (ay * tz - az * ty - bx),
            scale * (az * tx - ax * tz - by),
            scale * (ax * ty - ay * tx - bz),
            jnp.zeros((ROWS - 3, LANES), f32),
        ],
        axis=0,
    )


def place_quarters(outer, ways, angles, speeds, placed, result):
    per = LANES // angles
    me = lax.axis_index("tgt")
    for i, step in enumerate(line_order(outer)):
        if step < ways:
            placed[source_of(me, turn(step, ways), ways)] = speeds[i]
    result[...] = jnp.zeros(result.shape, f32)
    for k in range(ways // per):
        block = placed[k * per]
        for i in range(1, per):
            block = block + pltpu.roll(placed[k * per + i], i * angles, 1)
        result[3 * k : 3 * k + 3, :] = block[0:3]


def early_kernel(scale, outer, inner, count, *refs):
    messages, (after, speeds, moments, others, along, terms) = refs[:count], refs[count : count + 6]
    own_speeds, own_along, own_terms = refs[count + 6 :]
    middle = middle_of(outer, inner)
    angles = along.shape[2]
    for i, message in enumerate(messages):
        tile_terms(message, middle, moments.at[i], others.at[i])
        along[i], terms[i] = point_terms(message, angles, angles, middle)
        own_along[i], own_terms[i] = point_terms(message, 0, angles, middle)

    def one(i, unused):
        speeds[i] = quarter_speed(scale, along.at[i], terms[i], (moments, others))
        own_speeds[i] = quarter_speed(scale, own_along.at[i], own_terms[i], (moments, others))
        return unused

    repeat(count, one, 0)


def over_groups(scale, along, terms, groups, more):
    count = sum(others.shape[0] for moments, others, *rest in groups)
    if count <= UNROLLED:
        blocks = [
            (moments.at[i], others.at[i])
            for moments, others, *rest in groups
            for i in range(others.shape[0])
        ]
        return quarter_speed(scale, along, terms, blocks + more)
    total = quarter_speed(scale, along, terms, more)
    for moments, others, *rest in groups:
        total = total + quarter_speed(scale, along, terms, (moments, others))
    return total


def add_message(scale, middle, message, before, groups, moments, others, speeds):
    angles = groups[0][2].shape[2]
    tile_terms(message, middle, moments, others)
    along, terms = point_terms(message, angles, angles, middle)
    start = 0
    for there_moments, there_others, there_along, there_terms in groups:

        def one(i, unused, start=start, there_along=there_along, there_terms=there_terms):
            speeds[start + i] = before[start + i] + quarter_speed(
                scale, there_along.at[i], there_terms[i], [(moments, others)]
            )
            return unused

        repeat(there_others.shape[0], one, 0)
        start += there_others.shape[0]
    speeds[start] = over_groups(scale, along, terms, groups, [(moments, others)])
    return along, terms


def second_kernel(scale, outer, inner, *refs):
    message, before, *held, speeds, moments, others, along, terms = refs
    along[0], terms[0] = add_message(
        scale, middle_of(outer, inner), message, before, [held], moments.at[0], others.at[0], speeds
    )


def late_kernel(scale, ways, outer, inner, *refs):
    message, before = refs[:2]
    result, moments, others, speeds, placed = refs[10:]
    groups = [refs[2:6], refs[6:10]]
    add_message(scale, middle_of(outer, inner), message, before, groups, moments, others, speeds)
    place_quarters(outer, ways, groups[0][2].shape[2], speeds, placed, result)


def own_kernel(scale, ways, outer, inner, *refs):
    (*line, before, along, terms, moments, others, second_moments, second_others,
     last_moments, last_others, after, result, late_along, late_terms, speeds, placed) = refs
    second, last = (second_moments, second_others), [(last_moments, last_others)]
    middle = middle_of(outer, inner)
    angles = along.shape[2]
    early = before.shape[0]
    messages = line[early:]
    for i, message in enumerate(messages):
        late_along[i], late_terms[i] = point_terms(message, 0, angles, middle)

    def one(i, unused):
        speeds[i] = before[i] + over_groups(scale, along.at[i], terms[i], [second], last)
        return unused

    repeat(early, one, 0)
    for i in range(len(messages)):
        speeds[early + i] = over_groups(
            scale, late_along.at[i], late_terms[i], [(moments, others), second], last
        )
    place_quarters(outer, ways, angles, speeds, placed, result)


def prepare_kernel(ways, angles, blocks, *refs):
    messages = refs[:ways]
    after, inner_cells, index, placed = refs[ways:]
    me = lax.axis_index("tgt")
    for step, message in zip(tgt_order(ways), messages):
        placed[source_of(me, step, ways)] = message[0:5]

    cells = [
        jnp.concatenate([placed[t, c, :, 0:angles] for t in range(ways)], axis=1)
        for c in range(5)
    ]
    first = lax.broadcasted_iota(jnp.int32, cells[0].shape, 0) == 0
    for m, center in enumerate(inner_step(cells[0:3], cells[3], cells[4], [0.0] * 3, first)):
        inner_cells[m] = center
    inner_cells[3] = cells[3]
    inner_cells[4] = cells[4]

    shaped = (16 * ((blocks + 15) // 16), LANES)
    name = (me * blocks + lax.broadcasted_iota(jnp.int32, shaped, 0)).astype(f32)
    lane = lax.broadcasted_iota(jnp.int32, shaped, 1).astype(f32)
    row = jnp.full(shaped, -1.0, f32)
    slot = jnp.zeros(shaped, f32)
    for step, message in enumerate(messages):
        match = message[5, 1:2, :] == name
        row = jnp.maximum(row, jnp.where(match, message[5, 0:1, :], -1.0))
        slot = jnp.maximum(slot, jnp.where(match, lane + float(step * blocks), 0.0))
    row = jnp.max(row, axis=1, keepdims=True)
    slot = jnp.max(slot, axis=1, keepdims=True)
    block = lax.broadcasted_iota(jnp.int32, shaped, 0).astype(f32)
    kept = row < 0.0
    row = jnp.where(kept, float(3 * angles * ways) + block, row)
    slot = jnp.where(kept, float(ways * blocks) + block, slot)
    half = LANES // 2
    across = jnp.where(lane == block, row, 0.0) + jnp.where(lane == block + float(half), slot, 0.0)
    index[...] = jnp.sum(across, axis=0, keepdims=True).astype(jnp.int32)


def merge_kernel(rows, own, arrived, picks, result):
    result[...] = jnp.zeros(result.shape, f32)
    result[0:rows, :] = own[0:rows, :] + arrived[0:rows, :]
    result[rows : rows + picks.shape[0], :] = picks[...]


def wall_kernel(ways, *refs):
    partials = refs[:ways]
    (still, inner_cells, strength, index, wall, grid, new_strength,
     fixed, picked, halves, rows, sem) = refs[ways:]
    angles = grid.shape[2]
    total = angles * ways
    parts = total // LANES
    per = LANES // angles
    rows_of = 3 * parts
    pieces = strength.shape[1] // LANES
    slots = 3 * pieces
    me = lax.axis_index("tgt")
    copy = pltpu.make_async_copy(index, rows, sem)
    copy.start()
    places = [
        (b, b // pieces, slice((b % pieces) * LANES, (b % pieces + 1) * LANES))
        for b in range(3 * pieces)
    ]
    for step, partial in enumerate(partials):
        picked[step * slots : (step + 1) * slots, :] = partial[rows_of : rows_of + slots, :]
    for b, c, part in places:
        picked[ways * slots + b : ways * slots + b + 1, :] = strength[c : c + 1, part]
        fixed[3 * total + b : 3 * total + b + 1, :] = strength[c : c + 1, part]
    added = partials[0][0:rows_of, :]
    for partial in partials[1:]:
        added = added + partial[0:rows_of, :]
    speed = [
        jnp.concatenate([added[3 * k + m : 3 * k + m + 1] for k in range(parts)], axis=1)
        for m in range(3)
    ]
    for i in range(per):
        moved = added if i == 0 else pltpu.roll(added, LANES - i * angles, 1)
        for k in range(parts):
            halves[k * per + i, 0:3, :] = moved[3 * k : 3 * k + 3]
    for m in range(3):
        wall[m] = halves[me, m : m + 1, 0:angles]

    first = lax.broadcasted_iota(jnp.int32, (ROWS, total), 0) == 0
    local_swirl = inner_cells[3]
    local_diff = inner_cells[4]
    gain = jnp.where(first, local_diff, 0.0)
    field = [inner_cells[m] + gain * speed[m] for m in range(3)]
    for counter in range(1, SUBSTEPS):
        field = inner_step(field, local_swirl, local_diff, speed, first)
    stacked = jnp.concatenate(field + [jnp.zeros((LANES - 3 * ROWS, total), f32)], axis=0)
    for k in range(parts):
        turned = jnp.transpose(stacked[:, k * LANES : (k + 1) * LANES])
        for m in range(3):
            place = m * total + k * LANES
            fixed[place : place + LANES, :] = turned if m == 0 else pltpu.roll(
                turned, LANES - m * ROWS, 1
            )
    near = lax.broadcasted_iota(jnp.int32, (angles, LANES), 1) < SUBSTEPS
    for m in range(3):
        place = pl.multiple_of(m * total + me * angles, ROWS)
        grid[0, m] = jnp.where(near, fixed[pl.ds(place, angles), :], still[m])
    near = lax.broadcasted_iota(jnp.int32, (1, LANES), 1) < SUBSTEPS
    copy.wait()
    for b, c, part in places:
        new_strength[c : c + 1, part] = jnp.where(
            near, fixed[pl.ds(rows[0, b], 1), :], picked[pl.ds(rows[0, LANES // 2 + b], 1), :]
        )


def send(block, pairs):
    return lax.ppermute(block, ("src", "tgt"), pairs)


def on_device(
    particle_position,
    particle_strength,
    core_radius,
    boundary_points,
    vorticity,
    swirl,
    diffusivity,
    intersection_source,
    intersection_target,
):
    sources = lax.axis_size("src")
    ways = lax.axis_size("tgt")
    planes, comps, angles, radial = vorticity.shape
    per_device = particle_position.shape[1]
    tiles = per_device // LANES
    blocks = intersection_source.shape[2]
    inner = 2 if sources % 2 == 0 else 1
    outer = sources // inner
    total = angles * ways
    scale = 1.6 / (4.0 * math.pi * math.sqrt(per_device * ways * sources))

    def pairs(move):
        found = []
        for s in range(sources):
            for t in range(ways):
                o, i, u = move(s // inner, s % inner, t)
                found.append((s * ways + t, (o * inner + i) * ways + u))
        return found

    def over_tgt(block, step):
        return send(block, pairs(lambda o, i, t: (o, i, partner(t, step, ways))))

    given = (
        particle_position, particle_strength, core_radius, boundary_points,
        vorticity, swirl, diffusivity, intersection_source, intersection_target,
    )
    *messages, own, source, target = pl.pallas_call(
        functools.partial(particles_kernel, inner, outer),
        out_shape=(shape(tiles, ROWS, LANES),) * outer + (
            shape(5, angles, LANES),
            jax.ShapeDtypeStruct(intersection_source.shape, jnp.int32),
            jax.ShapeDtypeStruct(intersection_target.shape, jnp.int32),
        ),
        in_specs=[hbm()] * 9,
        out_specs=(vmem(),) * (outer + 3),
        scratch_shapes=[pltpu.VMEM(a.shape, f32) for a in given[0:4]]
        + [pltpu.SemaphoreType.DMA((11,))],
        compiler_params=limit(4),
        name="particles",
    )(*stay(*given))
    line = [messages[0]] + [
        send(
            message,
            pairs(lambda o, i, t: (partner(o, k, outer), i, partner(t, turn(k, ways), ways))),
        )
        for k, message in zip(line_order(outer)[1:], messages[1:])
    ]

    edges = pl.pallas_call(
        edges_kernel,
        out_shape=shape(11, ROWS, LANES),
        in_specs=[vmem()] * 3,
        out_specs=vmem(),
        compiler_params=limit(4),
        cost_estimate=cost(1 << 31, 1 << 10),
        name="edges",
    )(own, source, target)
    steps = tgt_order(ways)
    around = [edges] + [over_tgt(edges, k) for k in steps[1:]]

    rows = 3 * total // LANES
    slots = blocks
    sums_shape = shape(-(-rows // ROWS) * ROWS, LANES)
    along_shape = (ROWS, angles)
    terms_shape = (angles, TERMS)
    others_shape = (TERMS, per_device)
    early = outer - 2

    def held_shapes(count):
        return (
            shape(count, tiles, ROWS, LANES),
            jax.ShapeDtypeStruct((count, *others_shape), bf16),
            shape(count, *along_shape),
            jax.ShapeDtypeStruct((count, *terms_shape), bf16),
        )

    before, *held = pl.pallas_call(
        functools.partial(early_kernel, scale, outer, inner, early),
        out_shape=(
            shape(early, ROWS, LANES),
            *held_shapes(early),
            shape(early, ROWS, LANES),
            *held_shapes(early)[2:],
        ),
        in_specs=[vmem()] * (early + 1),
        out_specs=(vmem(),) * 8,
        compiler_params=limit(12),
        cost_estimate=cost(1 << 10, 1 << 10),
        name="early",
    )(*line[:early], edges)
    held, own_held = held[:4], held[4:]
    before, *second = pl.pallas_call(
        functools.partial(second_kernel, scale, outer, inner),
        out_shape=(shape(early + 1, ROWS, LANES), *held_shapes(1)),
        in_specs=[vmem()] * 6,
        out_specs=(vmem(),) * 5,
        compiler_params=limit(12),
        cost_estimate=cost(1 << 10, 1 << 10),
        name="second",
    )(line[early], before, *held)
    for_partner, last_moments, last_others = pl.pallas_call(
        functools.partial(late_kernel, scale, ways, outer, inner),
        out_shape=(
            sums_shape,
            shape(tiles, ROWS, LANES),
            jax.ShapeDtypeStruct(others_shape, bf16),
        ),
        in_specs=[vmem()] * 10,
        out_specs=(vmem(),) * 3,
        scratch_shapes=[
            pltpu.VMEM((outer, ROWS, LANES), f32),
            pltpu.VMEM((ways, ROWS, LANES), f32),
        ],
        compiler_params=limit(12),
        cost_estimate=cost(1 << 30, 1 << 10),
        name="late",
    )(line[-1], before, *held, *second)
    arrived = send(
        for_partner, pairs(lambda o, i, t: (o, inner - 1 - i, t ^ 1 if ways % 2 == 0 else t))
    )
    own_sum = pl.pallas_call(
        functools.partial(own_kernel, scale, ways, outer, inner),
        out_shape=sums_shape,
        in_specs=[vmem()] * (outer + 10),
        out_specs=vmem(),
        scratch_shapes=[
            pltpu.VMEM((2, *along_shape), f32),
            pltpu.VMEM((2, *terms_shape), bf16),
            pltpu.VMEM((outer, ROWS, LANES), f32),
            pltpu.VMEM((ways, ROWS, LANES), f32),
        ],
        compiler_params=limit(12),
        cost_estimate=cost(1 << 31, 1 << 10),
        name="own",
    )(
        *line, *own_held, *held[0:2], *second[0:2],
        last_moments, last_others, for_partner,
    )
    still, picks = pl.pallas_call(
        functools.partial(still_kernel, ways),
        out_shape=(
            shape(3, angles, LANES),
            shape(slots, LANES),
        ),
        in_specs=[vmem()] * (ways + 3),
        out_specs=(vmem(),) * 2,
        scratch_shapes=[
            pltpu.VMEM((ways, 5, ROWS, LANES), f32),
            pltpu.SMEM(source.shape, jnp.int32),
            pltpu.SemaphoreType.DMA,
        ],
        compiler_params=limit(8),
        name="still",
    )(*around, own, source, own_sum)
    partial_sum = pl.pallas_call(
        functools.partial(merge_kernel, rows),
        out_shape=shape(-(-(rows + blocks) // ROWS) * ROWS, LANES),
        in_specs=[vmem()] * 3,
        out_specs=vmem(),
        compiler_params=limit(4),
        name="merge",
    )(own_sum, arrived, picks)
    inner_cells, index = pl.pallas_call(
        functools.partial(prepare_kernel, ways, angles, blocks),
        out_shape=(
            shape(5, ROWS, total),
            jax.ShapeDtypeStruct((1, LANES), jnp.int32),
        ),
        in_specs=[vmem()] * (ways + 1),
        out_specs=(vmem(),) * 2,
        scratch_shapes=[pltpu.VMEM((ways, 5, ROWS, LANES), f32)],
        compiler_params=limit(8),
        name="prepare",
    )(*around, partial_sum)
    partials = [partial_sum] + [over_tgt(partial_sum, k) for k in steps[1:]]

    wall, grid, new_strength = pl.pallas_call(
        functools.partial(wall_kernel, ways),
        out_shape=(shape(3, planes, angles), shape(*vorticity.shape), shape(3, per_device)),
        in_specs=[vmem()] * (ways + 4),
        out_specs=(vmem(),) * 3,
        scratch_shapes=[
            pltpu.VMEM((3 * total + slots, LANES), f32),
            pltpu.VMEM((slots * ways + slots, LANES), f32),
            pltpu.VMEM((ways, ROWS, LANES), f32),
            pltpu.SMEM(index.shape, jnp.int32),
            pltpu.SemaphoreType.DMA,
        ],
        compiler_params=limit(16),
        name="wall",
    )(*partials, still, inner_cells, particle_strength, index)
    return (wall, grid, new_strength)


def solution(mesh):
    in_specs = (
        P(None, ("src", "tgt")),
        P(None, ("src", "tgt")),
        P(None, ("src", "tgt")),
        P(None, None, "tgt"),
        P("src", None, "tgt", None),
        P("src", "tgt", None),
        P("src", "tgt", None),
        P("src", "tgt", None),
        P("src", "tgt", None),
    )
    out_specs = (P(None, "src", "tgt"), P("src", None, "tgt", None), P(None, ("src", "tgt")))
    return jax.shard_map(
        on_device, mesh=mesh, in_specs=in_specs, out_specs=out_specs, check_vma=False
    )
```

profile of v0, /device:TPU:0, one launch (start us, length us, event | category | flops | bytes accessed | tf_op | source)
XLA Modules:
  0.0 21.1 jit_solution(8830361678492130847)
XLA Ops:
  0.6 1.0 %particles.1 = (f32[3,8,128]{2,1,0:T(8,128)S(1)}, f32[3,8,128]{2,1,0:T(8,128)S(1)}, f32[3,8,128]{2,1,0:T(8,128)S(1)}, f32[3,8,128]{2,1,0:T(8,128)S(1)}, f32[5,64...) custom-call(f32[3,384]{1,0:T(4,128)} %refs_0_.1, f32[3,384]{1,0:T(4,128)} %refs_6_.3, ...), custom_call_target="tpu_custom_call" | custom-call | tf_op jit(solution)/shard_map/particles/pallas_call | solution.py:563
  1.6 5.0 %collective-permute-start = (f32[3,8,128]{2,1,0:T(8,128)S(1)}, f32[3,8,128]{2,1,0:T(8,128)S(1)}, u32[]{:S(2)}, u32[]{:S(2)}) collective-permute-start(f32[3,8,128]{2,1,0:T(8,128)S(1)} %get-tuple-element.31), channel_id=1, source_target_pairs={{0,18},{1,19},{2,16},{3,17},{4,22},{5,23},{6,20},{7,21},{8,26},{9,... | collective-permute-start | bytes 36872 | tf_op jit(solution)/shard_map/ppermute | solution.py:523
  6.7 0.5 %collective-permute-start.1 = (f32[3,8,128]{2,1,0:T(8,128)S(1)}, f32[3,8,128]{2,1,0:T(8,128)S(1)}, u32[]{:S(2)}, u32[]{:S(2)}) collective-permute-start(f32[3,8,128]{2,1,0:T(8,128)S(1)} %get-tuple-element.32), channel_id=1, source_target_pairs={{0,25},{1,24},{2,27},{3,26},{4,29},{5,28},{6,31},{7,30},{8,17},{9,... | collective-permute-start | bytes 36872 | tf_op jit(solution)/shard_map/ppermute | solution.py:523
  7.2 0.2 collective-permute-start.2
  7.4 0.1 edges.1.refs_2_.refs_0_
  7.5 1.5 %collective-permute-start.4 = (f32[11,8,128]{2,1,0:T(8,128)S(1)}, f32[11,8,128]{2,1,0:T(8,128)S(1)}, u32[]{:S(2)}, u32[]{:S(2)}) collective-permute-start(f32[11,8,128]{2,1,0:T(8,128)S(1)} %edges.1.refs_2_.refs_0_), channel_id=1, source_target_pairs={{0,2},{1,3},{2,0},{3,1},{4,6},{5,7},{6,4},{7,5},{8,10},{9,11},{10,... | collective-permute-start | bytes 135176 | tf_op jit(solution)/shard_map/ppermute | solution.py:523
  9.0 0.8 %collective-permute-start.5 = (f32[11,8,128]{2,1,0:T(8,128)S(1)}, f32[11,8,128]{2,1,0:T(8,128)S(1)}, u32[]{:S(2)}, u32[]{:S(2)}) collective-permute-start(f32[11,8,128]{2,1,0:T(8,128)S(1)} %edges.1.refs_2_.refs_0_), channel_id=1, source_target_pairs={{0,3},{1,2},{2,1},{3,0},{4,7},{5,6},{6,5},{7,4},{8,11},{9,10},{10,... | collective-permute-start | bytes 135176 | tf_op jit(solution)/shard_map/ppermute | solution.py:523
  9.8 0.0 collective-permute-done.refs_1_
  9.8 0.0 collective-permute-start.6
  9.8 0.8 %early.1 = (f32[2,8,128]{2,1,0:T(8,128)S(1)}, f32[2,3,8,128]{3,2,1,0:T(8,128)S(1)}, bf16[2,48,384]{2,1,0:T(8,128)(2,1)S(1)}, f32[2,8,64]{2,1,0:T(8,128)S(1)}, bf...) custom-call(f32[3,8,128]{2,1,0:T(8,128)S(1)} %get-tuple-element.30.r, ...), custom_call_target="tpu_custom_call" | custom-call | flops 1024 | bytes 1024 | tf_op jit(solution)/shard_map/early/pallas_call | solution.py:613
  10.6 1.0 %collective-permute-done.1.refs_0_.refs_2_ = f32[3,8,128]{2,1,0:T(8,128)S(1)} collective-permute-done((f32[3,8,128]{2,1,0:T(8,128)S(1)}, f32[3,8,128]{2,1,0:T(8,128)S(1)}, u32[]{:S(2)}, u32[]{:S(2)}) %collective-permute-start.1) | collective-permute-done | bytes 12320 | tf_op jit(solution)/shard_map/ppermute | solution.py:523
  11.6 0.6 %second.1 = (f32[3,8,128]{2,1,0:T(8,128)S(1)}, f32[1,3,8,128]{3,2,1,0:T(8,128)S(1)}, bf16[1,48,384]{2,1,0:T(8,128)(2,1)S(1)}, f32[1,8,64]{2,1,0:T(8,128)S(1)}, bf16[1,64,48]{2,1,0:T(8,128)(2,1)S(1)}) custom-call(f32[3,8,128]{2,1,0:T(8,128)S(1)} %collective-permute-done.1.refs_0_.refs_2_, f32[2,8,128]{2,1,0:T(8,128)S(1)} %get-tuple-element.42.refs_1_, ...), custom_call_target="tpu_custom_call" | custom-call | flops 1024 | bytes 1024 | tf_op jit(solution)/shard_map/second/pallas_call | solution.py:628
  12.2 0.0 collective-permute-done.2.refs_0_.refs_3_
  12.2 0.7 %late.1 = (f32[8,128]{1,0:T(8,128)S(1)}, f32[3,8,128]{2,1,0:T(8,128)S(1)}, bf16[48,384]{1,0:T(8,128)(2,1)S(1)}) custom-call(f32[3,8,128]{2,1,0:T(8,128)S(1)} %collective-permute-done.2.refs_0_.refs_3_, f32[3,8,128]{2,1,0:T(8,128)S(1)} %get-tuple-element.47.refs_1_, f32[2,3,8,128]{3,2,1,0:T(8,128)S(1)} %get-tuple-element.40.refs_2_.refs_7_, ...), custom_call_target="tpu_custom_call" | custom-call | flops 1073741824 | bytes 1024 | tf_op jit(solution)/shard_map/late/pallas_call | solution.py:637
  12.9 1.2 %collective-permute-start.3 = (f32[8,128]{1,0:T(8,128)S(1)}, f32[8,128]{1,0:T(8,128)S(1)}, u32[]{:S(2)}, u32[]{:S(2)}) collective-permute-start(f32[8,128]{1,0:T(8,128)S(1)} %get-tuple-element.52.refs_13_), channel_id=1, source_target_pairs={{0,5},{1,4},{2,7},{3,6},{4,1},{5,0},{6,3},{7,2},{8,13},{9,12},{10,... | collective-permute-start | bytes 12296 | tf_op jit(solution)/shard_map/ppermute | solution.py:523
  14.1 1.0 %own.1.refs_6_ = f32[8,128]{1,0:T(8,128)S(1)} custom-call(f32[3,8,128]{2,1,0:T(8,128)S(1)} %get-tuple-element.30.refs_0_, f32[3,8,128]{2,1,0:T(8,128)S(1)} %collective-permute-done.refs_1_, f32[3,8,128]{2,1,0:T(8,128)S(1)} %collective-permute-done.1.refs_0_.refs_2_, f32[3,8,128]{2,1,0:T(8,128)S(1)} %collective-permute-done.2.refs_0_.refs_3_, ...), custom_call_target="tpu_custom_call" | custom-call | flops 2147483648 | bytes 1024 | tf_op jit(solution)/shard_map/own/pallas_call | solution.py:657
  15.1 0.0 collective-permute-done.4.refs_1_
  15.1 0.0 collective-permute-done.5.refs_2_
  15.1 0.0 collective-permute-done.6.refs_3_
  15.1 0.6 %still.1 = (f32[3,64,128]{2,1,0:T(8,128)S(1)}, f32[9,128]{1,0:T(8,128)S(1)}) custom-call(f32[11,8,128]{2,1,0:T(8,128)S(1)} %edges.1.refs_2_.refs_0_, f32[11,8,128]{2,1,0:T(8,128)S(1)} %collective-permute-done.4.refs_1_, f32[11,8,128]{2,1,0:T(8,128)S(1)} %collective-permute-done.5.refs_2_, f32[11,8,128]{2,1,0:T(8,128)S(1)} %collective-permute-done.6.refs_3_, ...), custom_call_target="tpu_custom_call" | custom-call | tf_op jit(solution)/shard_map/still/pallas_call | solution.py:675
  15.7 0.2 collective-permute-done.3.arrived
  15.9 0.9 %collective-permute-start.7 = (f32[16,128]{1,0:T(8,128)S(1)}, f32[16,128]{1,0:T(8,128)S(1)}, u32[]{:S(2)}, u32[]{:S(2)}) collective-permute-start(f32[16,128]{1,0:T(8,128)S(1)} %merge.1.refs_4_.refs_0_), channel_id=1, source_target_pairs={{0,2},{1,3},{2,0},{3,1},{4,6},{5,7},{6,4},{7,5},{8,10},{9,11},{10,... | collective-permute-start | bytes 24584 | tf_op jit(solution)/shard_map/ppermute | solution.py:523
  16.8 0.8 %collective-permute-start.8 = (f32[16,128]{1,0:T(8,128)S(1)}, f32[16,128]{1,0:T(8,128)S(1)}, u32[]{:S(2)}, u32[]{:S(2)}) collective-permute-start(f32[16,128]{1,0:T(8,128)S(1)} %merge.1.refs_4_.refs_0_), channel_id=1, source_target_pairs={{0,3},{1,2},{2,1},{3,0},{4,7},{5,6},{6,5},{7,4},{8,11},{9,10},{10,... | collective-permute-start | bytes 24584 | tf_op jit(solution)/shard_map/ppermute | solution.py:523
  17.6 0.5 %collective-permute-start.9 = (f32[16,128]{1,0:T(8,128)S(1)}, f32[16,128]{1,0:T(8,128)S(1)}, u32[]{:S(2)}, u32[]{:S(2)}) collective-permute-start(f32[16,128]{1,0:T(8,128)S(1)} %merge.1.refs_4_.refs_0_), channel_id=1, source_target_pairs={{0,1},{1,0},{2,3},{3,2},{4,5},{5,4},{6,7},{7,6},{8,9},{9,8},{10,11... | collective-permute-start | bytes 24584 | tf_op jit(solution)/shard_map/ppermute | solution.py:523
  18.1 0.0 copy-start
  18.1 0.2 prepare.1
  18.3 1.3 %collective-permute-done.7.refs_1_ = f32[16,128]{1,0:T(8,128)S(1)} collective-permute-done((f32[16,128]{1,0:T(8,128)S(1)}, f32[16,128]{1,0:T(8,128)S(1)}, u32[]{:S(2)}, u32[]{:S(2)}) %collective-permute-start.7) | collective-permute-done | bytes 8224 | tf_op jit(solution)/shard_map/ppermute | solution.py:523
  19.6 0.3 %collective-permute-done.8.refs_2_ = f32[16,128]{1,0:T(8,128)S(1)} collective-permute-done((f32[16,128]{1,0:T(8,128)S(1)}, f32[16,128]{1,0:T(8,128)S(1)}, u32[]{:S(2)}, u32[]{:S(2)}) %collective-permute-start.8) | collective-permute-done | bytes 8224 | tf_op jit(solution)/shard_map/ppermute | solution.py:523
  19.9 0.0 collective-permute-done.9.refs_3_
  19.9 0.0 copy-done
  19.9 1.2 %wall.1 = (f32[3,1,64]{2,1,0:T(1,128)}, f32[1,3,64,128]{3,2,1,0:T(8,128)}, f32[3,384]{1,0:T(4,128)}) custom-call(f32[16,128]{1,0:T(8,128)S(1)} %merge.1.refs_4_.refs_0_, f32[16,128]{1,0:T(8,128)S(1)} %collective-permute-done.7.refs_1_, f32[16,128]{1,0:T(8,128)S(1)} %collective-permute-done.8.refs_2_, f32[16,128]{1,0:T(8,128)S(1)} %collective-permute-done.9.refs_3_, ...), custom_call_target="tpu_custom_call" | custom-call | tf_op jit(solution)/shard_map/wall/pallas_call | solution.py:713
  (1 shorter events, 0.0 us)
Async XLA Ops:
  1.6 8.2 %collective-permute-start = (f32[3,8,128]{2,1,0:T(8,128)S(1)}, f32[3,8,128]{2,1,0:T(8,128)S(1)}, u32[]{:S(2)}, u32[]{:S(2)}) collective-permute-start(f32[3,8,128]{2,1,0:T(8,128)S(1)} %get-tuple-element.31), channel_id=1, source_target_pairs={{0,18},{1,19},{2,16},{3,17},{4,22},{5,23},{6,20},{7,21},{8,26},{9,... | collective-permute-start | bytes 36872 | tf_op jit(solution)/shard_map/ppermute | solution.py:523
  6.7 4.9 %collective-permute-start.1 = (f32[3,8,128]{2,1,0:T(8,128)S(1)}, f32[3,8,128]{2,1,0:T(8,128)S(1)}, u32[]{:S(2)}, u32[]{:S(2)}) collective-permute-start(f32[3,8,128]{2,1,0:T(8,128)S(1)} %get-tuple-element.32), channel_id=1, source_target_pairs={{0,25},{1,24},{2,27},{3,26},{4,29},{5,28},{6,31},{7,30},{8,17},{9,... | collective-permute-start | bytes 36872 | tf_op jit(solution)/shard_map/ppermute | solution.py:523
  7.2 5.0 %collective-permute-start.2 = (f32[3,8,128]{2,1,0:T(8,128)S(1)}, f32[3,8,128]{2,1,0:T(8,128)S(1)}, u32[]{:S(2)}, u32[]{:S(2)}) collective-permute-start(f32[3,8,128]{2,1,0:T(8,128)S(1)} %get-tuple-element.33), channel_id=1, source_target_pairs={{0,11},{1,10},{2,9},{3,8},{4,15},{5,14},{6,13},{7,12},{8,3},{9,2},... | collective-permute-start | bytes 36872 | tf_op jit(solution)/shard_map/ppermute | solution.py:523
  7.5 7.6 %collective-permute-start.4 = (f32[11,8,128]{2,1,0:T(8,128)S(1)}, f32[11,8,128]{2,1,0:T(8,128)S(1)}, u32[]{:S(2)}, u32[]{:S(2)}) collective-permute-start(f32[11,8,128]{2,1,0:T(8,128)S(1)} %edges.1.refs_2_.refs_0_), channel_id=1, source_target_pairs={{0,2},{1,3},{2,0},{3,1},{4,6},{5,7},{6,4},{7,5},{8,10},{9,11},{10,... | collective-permute-start | bytes 135176 | tf_op jit(solution)/shard_map/ppermute | solution.py:523
  9.0 6.1 %collective-permute-start.5 = (f32[11,8,128]{2,1,0:T(8,128)S(1)}, f32[11,8,128]{2,1,0:T(8,128)S(1)}, u32[]{:S(2)}, u32[]{:S(2)}) collective-permute-start(f32[11,8,128]{2,1,0:T(8,128)S(1)} %edges.1.refs_2_.refs_0_), channel_id=1, source_target_pairs={{0,3},{1,2},{2,1},{3,0},{4,7},{5,6},{6,5},{7,4},{8,11},{9,10},{10,... | collective-permute-start | bytes 135176 | tf_op jit(solution)/shard_map/ppermute | solution.py:523
  9.8 5.3 %collective-permute-start.6 = (f32[11,8,128]{2,1,0:T(8,128)S(1)}, f32[11,8,128]{2,1,0:T(8,128)S(1)}, u32[]{:S(2)}, u32[]{:S(2)}) collective-permute-start(f32[11,8,128]{2,1,0:T(8,128)S(1)} %edges.1.refs_2_.refs_0_), channel_id=1, source_target_pairs={{0,1},{1,0},{2,3},{3,2},{4,5},{5,4},{6,7},{7,6},{8,9},{9,8},{10,11... | collective-permute-start | bytes 135176 | tf_op jit(solution)/shard_map/ppermute | solution.py:523
  12.9 3.0 %collective-permute-start.3 = (f32[8,128]{1,0:T(8,128)S(1)}, f32[8,128]{1,0:T(8,128)S(1)}, u32[]{:S(2)}, u32[]{:S(2)}) collective-permute-start(f32[8,128]{1,0:T(8,128)S(1)} %get-tuple-element.52.refs_13_), channel_id=1, source_target_pairs={{0,5},{1,4},{2,7},{3,6},{4,1},{5,0},{6,3},{7,2},{8,13},{9,12},{10,... | collective-permute-start | bytes 12296 | tf_op jit(solution)/shard_map/ppermute | solution.py:523
  15.9 3.7 %collective-permute-start.7 = (f32[16,128]{1,0:T(8,128)S(1)}, f32[16,128]{1,0:T(8,128)S(1)}, u32[]{:S(2)}, u32[]{:S(2)}) collective-permute-start(f32[16,128]{1,0:T(8,128)S(1)} %merge.1.refs_4_.refs_0_), channel_id=1, source_target_pairs={{0,2},{1,3},{2,0},{3,1},{4,6},{5,7},{6,4},{7,5},{8,10},{9,11},{10,... | collective-permute-start | bytes 24584 | tf_op jit(solution)/shard_map/ppermute | solution.py:523
  16.8 3.1 %collective-permute-start.8 = (f32[16,128]{1,0:T(8,128)S(1)}, f32[16,128]{1,0:T(8,128)S(1)}, u32[]{:S(2)}, u32[]{:S(2)}) collective-permute-start(f32[16,128]{1,0:T(8,128)S(1)} %merge.1.refs_4_.refs_0_), channel_id=1, source_target_pairs={{0,3},{1,2},{2,1},{3,0},{4,7},{5,6},{6,5},{7,4},{8,11},{9,10},{10,... | collective-permute-start | bytes 24584 | tf_op jit(solution)/shard_map/ppermute | solution.py:523
  17.6 2.3 %collective-permute-start.9 = (f32[16,128]{1,0:T(8,128)S(1)}, f32[16,128]{1,0:T(8,128)S(1)}, u32[]{:S(2)}, u32[]{:S(2)}) collective-permute-start(f32[16,128]{1,0:T(8,128)S(1)} %merge.1.refs_4_.refs_0_), channel_id=1, source_target_pairs={{0,1},{1,0},{2,3},{3,2},{4,5},{5,4},{6,7},{7,6},{8,9},{9,8},{10,11... | collective-permute-start | bytes 24584 | tf_op jit(solution)/shard_map/ppermute | solution.py:523
  18.1 1.8 %copy-start = (f32[3,384]{1,0:T(4,128)S(1)}, f32[3,384]{1,0:T(4,128)}, u32[]{:S(2)}) copy-start(f32[3,384]{1,0:T(4,128)} %refs_6_.3) | copy-start | bytes 13828
where the time goes:
time: 21.3 us; the launch traced here: 21.1 us
  starting transfers between devices  11.4 us (54%)
  Pallas kernels  6.19 us (29%)
  waiting for transfers between devices  2.8 us (13%)
  between operations  0.69 us (3%)
    ppermute x10, starting transfers between devices, send(): return lax.ppermute(block, ('src', 'tgt'), pairs)  11.4 us
    ppermute x10, waiting for transfers between devices, send(): return lax.ppermute(block, ('src', 'tgt'), pairs)  2.8 us
    pallas_call x1, Pallas kernels, on_device(): pl.pallas_call(functools.partial(wall_kernel, ways), out_shape=(shape(3,...  1.21 us
    pallas_call x1, Pallas kernels, on_device(): pl.pallas_call(functools.partial(particles_kernel, inner, outer), out_sha...  0.99 us
    pallas_call x1, Pallas kernels, on_device(): pl.pallas_call(functools.partial(own_kernel, scale, ways, outer, inner),...  0.97 us
    pallas_call x1, Pallas kernels, on_device(): pl.pallas_call(functools.partial(early_kernel, scale, outer, inner, early...  0.82 us
    pallas_call x1, Pallas kernels, on_device(): pl.pallas_call(functools.partial(late_kernel, scale, ways, outer, inner),...  0.73 us
    pallas_call x1, Pallas kernels, on_device(): pl.pallas_call(functools.partial(still_kernel, ways), out_shape=(shape(3,...  0.63 us
  transfers between devices with their start and end apart: 10, of which 4 were waited for; matrix products, arithmetic and copies ran while one was open for 0% of the time, Pallas kernels for 19%

commit v1 on v0

--- a/solution.py
+++ b/solution.py
@@ -11,7 +11,7 @@
 SUBSTEPS = 3
 LANES = 128
 ROWS = 8
-TOGETHER = 2
+TOGETHER = 4
 TERMS = 48
 UNROLLED = 4
 swirl_gain = 0.2

time: 21.3 us -> 21.3 us (level)
  no operation moved by 1% of the time
where the time goes in v1:
time: 21.3 us; the launch traced here: 21.1 us
  starting transfers between devices  11.4 us (54%)
  Pallas kernels  6.19 us (29%)
  waiting for transfers between devices  2.8 us (13%)
  between operations  0.69 us (3%)
    ppermute x10, starting transfers between devices, send(): return lax.ppermute(block, ('src', 'tgt'), pairs)  11.4 us
    ppermute x10, waiting for transfers between devices, send(): return lax.ppermute(block, ('src', 'tgt'), pairs)  2.8 us
    pallas_call x1, Pallas kernels, on_device(): pl.pallas_call(functools.partial(wall_kernel, ways), out_shape=(shape(3,...  1.21 us
    pallas_call x1, Pallas kernels, on_device(): pl.pallas_call(functools.partial(particles_kernel, inner, outer), out_sha...  0.99 us
    pallas_call x1, Pallas kernels, on_device(): pl.pallas_call(functools.partial(own_kernel, scale, ways, outer, inner),...  0.97 us
    pallas_call x1, Pallas kernels, on_device(): pl.pallas_call(functools.partial(early_kernel, scale, outer, inner, early...  0.82 us
    pallas_call x1, Pallas kernels, on_device(): pl.pallas_call(functools.partial(late_kernel, scale, ways, outer, inner),...  0.73 us
    pallas_call x1, Pallas kernels, on_device(): pl.pallas_call(functools.partial(still_kernel, ways), out_shape=(shape(3,...  0.63 us
  transfers between devices with their start and end apart: 10, of which 4 were waited for; matrix products, arithmetic and copies ran while one was open for 0% of the time, Pallas kernels for 19%

profile of v1, /device:TPU:0, one launch (start us, length us, event | category | flops | bytes accessed | tf_op | source)
XLA Modules:
  0.0 21.1 jit_solution(7267824581242868066)
XLA Ops:
  0.6 1.0 %particles.1 = (f32[3,8,128]{2,1,0:T(8,128)S(1)}, f32[3,8,128]{2,1,0:T(8,128)S(1)}, f32[3,8,128]{2,1,0:T(8,128)S(1)}, f32[3,8,128]{2,1,0:T(8,128)S(1)}, f32[5,64...) custom-call(f32[3,384]{1,0:T(4,128)} %refs_0_.1, f32[3,384]{1,0:T(4,128)} %refs_6_.3, ...), custom_call_target="tpu_custom_call" | custom-call | tf_op jit(solution)/shard_map/particles/pallas_call | solution.py:563
  1.6 5.0 %collective-permute-start = (f32[3,8,128]{2,1,0:T(8,128)S(1)}, f32[3,8,128]{2,1,0:T(8,128)S(1)}, u32[]{:S(2)}, u32[]{:S(2)}) collective-permute-start(f32[3,8,128]{2,1,0:T(8,128)S(1)} %get-tuple-element.31), channel_id=1, source_target_pairs={{0,18},{1,19},{2,16},{3,17},{4,22},{5,23},{6,20},{7,21},{8,26},{9,... | collective-permute-start | bytes 36872 | tf_op jit(solution)/shard_map/ppermute | solution.py:523
  6.7 0.5 %collective-permute-start.1 = (f32[3,8,128]{2,1,0:T(8,128)S(1)}, f32[3,8,128]{2,1,0:T(8,128)S(1)}, u32[]{:S(2)}, u32[]{:S(2)}) collective-permute-start(f32[3,8,128]{2,1,0:T(8,128)S(1)} %get-tuple-element.32), channel_id=1, source_target_pairs={{0,25},{1,24},{2,27},{3,26},{4,29},{5,28},{6,31},{7,30},{8,17},{9,... | collective-permute-start | bytes 36872 | tf_op jit(solution)/shard_map/ppermute | solution.py:523
  7.2 0.2 collective-permute-start.2
  7.4 0.1 edges.1.refs_2_.refs_0_
  7.5 1.5 %collective-permute-start.4 = (f32[11,8,128]{2,1,0:T(8,128)S(1)}, f32[11,8,128]{2,1,0:T(8,128)S(1)}, u32[]{:S(2)}, u32[]{:S(2)}) collective-permute-start(f32[11,8,128]{2,1,0:T(8,128)S(1)} %edges.1.refs_2_.refs_0_), channel_id=1, source_target_pairs={{0,2},{1,3},{2,0},{3,1},{4,6},{5,7},{6,4},{7,5},{8,10},{9,11},{10,... | collective-permute-start | bytes 135176 | tf_op jit(solution)/shard_map/ppermute | solution.py:523
  9.0 0.8 %collective-permute-start.5 = (f32[11,8,128]{2,1,0:T(8,128)S(1)}, f32[11,8,128]{2,1,0:T(8,128)S(1)}, u32[]{:S(2)}, u32[]{:S(2)}) collective-permute-start(f32[11,8,128]{2,1,0:T(8,128)S(1)} %edges.1.refs_2_.refs_0_), channel_id=1, source_target_pairs={{0,3},{1,2},{2,1},{3,0},{4,7},{5,6},{6,5},{7,4},{8,11},{9,10},{10,... | collective-permute-start | bytes 135176 | tf_op jit(solution)/shard_map/ppermute | solution.py:523
  9.8 0.0 collective-permute-done.refs_1_
  9.8 0.0 collective-permute-start.6
  9.8 0.8 %early.1 = (f32[2,8,128]{2,1,0:T(8,128)S(1)}, f32[2,3,8,128]{3,2,1,0:T(8,128)S(1)}, bf16[2,48,384]{2,1,0:T(8,128)(2,1)S(1)}, f32[2,8,64]{2,1,0:T(8,128)S(1)}, bf...) custom-call(f32[3,8,128]{2,1,0:T(8,128)S(1)} %get-tuple-element.30.r, ...), custom_call_target="tpu_custom_call" | custom-call | flops 1024 | bytes 1024 | tf_op jit(solution)/shard_map/early/pallas_call | solution.py:613
  10.6 1.0 %collective-permute-done.1.refs_0_.refs_2_ = f32[3,8,128]{2,1,0:T(8,128)S(1)} collective-permute-done((f32[3,8,128]{2,1,0:T(8,128)S(1)}, f32[3,8,128]{2,1,0:T(8,128)S(1)}, u32[]{:S(2)}, u32[]{:S(2)}) %collective-permute-start.1) | collective-permute-done | bytes 12320 | tf_op jit(solution)/shard_map/ppermute | solution.py:523
  11.6 0.6 %second.1 = (f32[3,8,128]{2,1,0:T(8,128)S(1)}, f32[1,3,8,128]{3,2,1,0:T(8,128)S(1)}, bf16[1,48,384]{2,1,0:T(8,128)(2,1)S(1)}, f32[1,8,64]{2,1,0:T(8,128)S(1)}, bf16[1,64,48]{2,1,0:T(8,128)(2,1)S(1)}) custom-call(f32[3,8,128]{2,1,0:T(8,128)S(1)} %collective-permute-done.1.refs_0_.refs_2_, f32[2,8,128]{2,1,0:T(8,128)S(1)} %get-tuple-element.42.refs_1_, ...), custom_call_target="tpu_custom_call" | custom-call | flops 1024 | bytes 1024 | tf_op jit(solution)/shard_map/second/pallas_call | solution.py:628
  12.2 0.0 collective-permute-done.2.refs_0_.refs_3_
  12.2 0.7 %late.1 = (f32[8,128]{1,0:T(8,128)S(1)}, f32[3,8,128]{2,1,0:T(8,128)S(1)}, bf16[48,384]{1,0:T(8,128)(2,1)S(1)}) custom-call(f32[3,8,128]{2,1,0:T(8,128)S(1)} %collective-permute-done.2.refs_0_.refs_3_, f32[3,8,128]{2,1,0:T(8,128)S(1)} %get-tuple-element.47.refs_1_, f32[2,3,8,128]{3,2,1,0:T(8,128)S(1)} %get-tuple-element.40.refs_2_.refs_7_, ...), custom_call_target="tpu_custom_call" | custom-call | flops 1073741824 | bytes 1024 | tf_op jit(solution)/shard_map/late/pallas_call | solution.py:637
  12.9 1.2 %collective-permute-start.3 = (f32[8,128]{1,0:T(8,128)S(1)}, f32[8,128]{1,0:T(8,128)S(1)}, u32[]{:S(2)}, u32[]{:S(2)}) collective-permute-start(f32[8,128]{1,0:T(8,128)S(1)} %get-tuple-element.52.refs_13_), channel_id=1, source_target_pairs={{0,5},{1,4},{2,7},{3,6},{4,1},{5,0},{6,3},{7,2},{8,13},{9,12},{10,... | collective-permute-start | bytes 12296 | tf_op jit(solution)/shard_map/ppermute | solution.py:523
  14.1 1.0 %own.1.refs_6_ = f32[8,128]{1,0:T(8,128)S(1)} custom-call(f32[3,8,128]{2,1,0:T(8,128)S(1)} %get-tuple-element.30.refs_0_, f32[3,8,128]{2,1,0:T(8,128)S(1)} %collective-permute-done.refs_1_, f32[3,8,128]{2,1,0:T(8,128)S(1)} %collective-permute-done.1.refs_0_.refs_2_, f32[3,8,128]{2,1,0:T(8,128)S(1)} %collective-permute-done.2.refs_0_.refs_3_, ...), custom_call_target="tpu_custom_call" | custom-call | flops 2147483648 | bytes 1024 | tf_op jit(solution)/shard_map/own/pallas_call | solution.py:657
  15.1 0.0 collective-permute-done.4.refs_1_
  15.1 0.0 collective-permute-done.5.refs_2_
  15.1 0.0 collective-permute-done.6.refs_3_
  15.1 0.6 %still.1 = (f32[3,64,128]{2,1,0:T(8,128)S(1)}, f32[9,128]{1,0:T(8,128)S(1)}) custom-call(f32[11,8,128]{2,1,0:T(8,128)S(1)} %edges.1.refs_2_.refs_0_, f32[11,8,128]{2,1,0:T(8,128)S(1)} %collective-permute-done.4.refs_1_, f32[11,8,128]{2,1,0:T(8,128)S(1)} %collective-permute-done.5.refs_2_, f32[11,8,128]{2,1,0:T(8,128)S(1)} %collective-permute-done.6.refs_3_, ...), custom_call_target="tpu_custom_call" | custom-call | tf_op jit(solution)/shard_map/still/pallas_call | solution.py:675
  15.7 0.2 %collective-permute-done.3.arrived = f32[8,128]{1,0:T(8,128)S(1)} collective-permute-done((f32[8,128]{1,0:T(8,128)S(1)}, f32[8,128]{1,0:T(8,128)S(1)}, u32[]{:S(2)}, u32[]{:S(2)}) %collective-permute-start.3) | collective-permute-done | bytes 4128 | tf_op jit(solution)/shard_map/ppermute | solution.py:523
  15.9 0.9 %collective-permute-start.7 = (f32[16,128]{1,0:T(8,128)S(1)}, f32[16,128]{1,0:T(8,128)S(1)}, u32[]{:S(2)}, u32[]{:S(2)}) collective-permute-start(f32[16,128]{1,0:T(8,128)S(1)} %merge.1.refs_4_.refs_0_), channel_id=1, source_target_pairs={{0,2},{1,3},{2,0},{3,1},{4,6},{5,7},{6,4},{7,5},{8,10},{9,11},{10,... | collective-permute-start | bytes 24584 | tf_op jit(solution)/shard_map/ppermute | solution.py:523
  16.8 0.8 %collective-permute-start.8 = (f32[16,128]{1,0:T(8,128)S(1)}, f32[16,128]{1,0:T(8,128)S(1)}, u32[]{:S(2)}, u32[]{:S(2)}) collective-permute-start(f32[16,128]{1,0:T(8,128)S(1)} %merge.1.refs_4_.refs_0_), channel_id=1, source_target_pairs={{0,3},{1,2},{2,1},{3,0},{4,7},{5,6},{6,5},{7,4},{8,11},{9,10},{10,... | collective-permute-start | bytes 24584 | tf_op jit(solution)/shard_map/ppermute | solution.py:523
  17.6 0.5 %collective-permute-start.9 = (f32[16,128]{1,0:T(8,128)S(1)}, f32[16,128]{1,0:T(8,128)S(1)}, u32[]{:S(2)}, u32[]{:S(2)}) collective-permute-start(f32[16,128]{1,0:T(8,128)S(1)} %merge.1.refs_4_.refs_0_), channel_id=1, source_target_pairs={{0,1},{1,0},{2,3},{3,2},{4,5},{5,4},{6,7},{7,6},{8,9},{9,8},{10,11... | collective-permute-start | bytes 24584 | tf_op jit(solution)/shard_map/ppermute | solution.py:523
  18.1 0.0 copy-start
  18.1 0.2 prepare.1
  18.3 1.3 %collective-permute-done.7.refs_1_ = f32[16,128]{1,0:T(8,128)S(1)} collective-permute-done((f32[16,128]{1,0:T(8,128)S(1)}, f32[16,128]{1,0:T(8,128)S(1)}, u32[]{:S(2)}, u32[]{:S(2)}) %collective-permute-start.7) | collective-permute-done | bytes 8224 | tf_op jit(solution)/shard_map/ppermute | solution.py:523
  19.6 0.3 %collective-permute-done.8.refs_2_ = f32[16,128]{1,0:T(8,128)S(1)} collective-permute-done((f32[16,128]{1,0:T(8,128)S(1)}, f32[16,128]{1,0:T(8,128)S(1)}, u32[]{:S(2)}, u32[]{:S(2)}) %collective-permute-start.8) | collective-permute-done | bytes 8224 | tf_op jit(solution)/shard_map/ppermute | solution.py:523
  19.9 0.0 collective-permute-done.9.refs_3_
  19.9 0.0 copy-done
  19.9 1.2 %wall.1 = (f32[3,1,64]{2,1,0:T(1,128)}, f32[1,3,64,128]{3,2,1,0:T(8,128)}, f32[3,384]{1,0:T(4,128)}) custom-call(f32[16,128]{1,0:T(8,128)S(1)} %merge.1.refs_4_.refs_0_, f32[16,128]{1,0:T(8,128)S(1)} %collective-permute-done.7.refs_1_, f32[16,128]{1,0:T(8,128)S(1)} %collective-permute-done.8.refs_2_, f32[16,128]{1,0:T(8,128)S(1)} %collective-permute-done.9.refs_3_, ...), custom_call_target="tpu_custom_call" | custom-call | tf_op jit(solution)/shard_map/wall/pallas_call | solution.py:713
  (1 shorter events, 0.0 us)
Async XLA Ops:
  1.6 8.2 %collective-permute-start = (f32[3,8,128]{2,1,0:T(8,128)S(1)}, f32[3,8,128]{2,1,0:T(8,128)S(1)}, u32[]{:S(2)}, u32[]{:S(2)}) collective-permute-start(f32[3,8,128]{2,1,0:T(8,128)S(1)} %get-tuple-element.31), channel_id=1, source_target_pairs={{0,18},{1,19},{2,16},{3,17},{4,22},{5,23},{6,20},{7,21},{8,26},{9,... | collective-permute-start | bytes 36872 | tf_op jit(solution)/shard_map/ppermute | solution.py:523
  6.7 4.9 %collective-permute-start.1 = (f32[3,8,128]{2,1,0:T(8,128)S(1)}, f32[3,8,128]{2,1,0:T(8,128)S(1)}, u32[]{:S(2)}, u32[]{:S(2)}) collective-permute-start(f32[3,8,128]{2,1,0:T(8,128)S(1)} %get-tuple-element.32), channel_id=1, source_target_pairs={{0,25},{1,24},{2,27},{3,26},{4,29},{5,28},{6,31},{7,30},{8,17},{9,... | collective-permute-start | bytes 36872 | tf_op jit(solution)/shard_map/ppermute | solution.py:523
  7.2 5.0 %collective-permute-start.2 = (f32[3,8,128]{2,1,0:T(8,128)S(1)}, f32[3,8,128]{2,1,0:T(8,128)S(1)}, u32[]{:S(2)}, u32[]{:S(2)}) collective-permute-start(f32[3,8,128]{2,1,0:T(8,128)S(1)} %get-tuple-element.33), channel_id=1, source_target_pairs={{0,11},{1,10},{2,9},{3,8},{4,15},{5,14},{6,13},{7,12},{8,3},{9,2},... | collective-permute-start | bytes 36872 | tf_op jit(solution)/shard_map/ppermute | solution.py:523
  7.5 7.6 %collective-permute-start.4 = (f32[11,8,128]{2,1,0:T(8,128)S(1)}, f32[11,8,128]{2,1,0:T(8,128)S(1)}, u32[]{:S(2)}, u32[]{:S(2)}) collective-permute-start(f32[11,8,128]{2,1,0:T(8,128)S(1)} %edges.1.refs_2_.refs_0_), channel_id=1, source_target_pairs={{0,2},{1,3},{2,0},{3,1},{4,6},{5,7},{6,4},{7,5},{8,10},{9,11},{10,... | collective-permute-start | bytes 135176 | tf_op jit(solution)/shard_map/ppermute | solution.py:523
  9.0 6.1 %collective-permute-start.5 = (f32[11,8,128]{2,1,0:T(8,128)S(1)}, f32[11,8,128]{2,1,0:T(8,128)S(1)}, u32[]{:S(2)}, u32[]{:S(2)}) collective-permute-start(f32[11,8,128]{2,1,0:T(8,128)S(1)} %edges.1.refs_2_.refs_0_), channel_id=1, source_target_pairs={{0,3},{1,2},{2,1},{3,0},{4,7},{5,6},{6,5},{7,4},{8,11},{9,10},{10,... | collective-permute-start | bytes 135176 | tf_op jit(solution)/shard_map/ppermute | solution.py:523
  9.8 5.3 %collective-permute-start.6 = (f32[11,8,128]{2,1,0:T(8,128)S(1)}, f32[11,8,128]{2,1,0:T(8,128)S(1)}, u32[]{:S(2)}, u32[]{:S(2)}) collective-permute-start(f32[11,8,128]{2,1,0:T(8,128)S(1)} %edges.1.refs_2_.refs_0_), channel_id=1, source_target_pairs={{0,1},{1,0},{2,3},{3,2},{4,5},{5,4},{6,7},{7,6},{8,9},{9,8},{10,11... | collective-permute-start | bytes 135176 | tf_op jit(solution)/shard_map/ppermute | solution.py:523
  12.9 3.0 %collective-permute-start.3 = (f32[8,128]{1,0:T(8,128)S(1)}, f32[8,128]{1,0:T(8,128)S(1)}, u32[]{:S(2)}, u32[]{:S(2)}) collective-permute-start(f32[8,128]{1,0:T(8,128)S(1)} %get-tuple-element.52.refs_13_), channel_id=1, source_target_pairs={{0,5},{1,4},{2,7},{3,6},{4,1},{5,0},{6,3},{7,2},{8,13},{9,12},{10,... | collective-permute-start | bytes 12296 | tf_op jit(solution)/shard_map/ppermute | solution.py:523
  15.9 3.7 %collective-permute-start.7 = (f32[16,128]{1,0:T(8,128)S(1)}, f32[16,128]{1,0:T(8,128)S(1)}, u32[]{:S(2)}, u32[]{:S(2)}) collective-permute-start(f32[16,128]{1,0:T(8,128)S(1)} %merge.1.refs_4_.refs_0_), channel_id=1, source_target_pairs={{0,2},{1,3},{2,0},{3,1},{4,6},{5,7},{6,4},{7,5},{8,10},{9,11},{10,... | collective-permute-start | bytes 24584 | tf_op jit(solution)/shard_map/ppermute | solution.py:523
  16.8 3.1 %collective-permute-start.8 = (f32[16,128]{1,0:T(8,128)S(1)}, f32[16,128]{1,0:T(8,128)S(1)}, u32[]{:S(2)}, u32[]{:S(2)}) collective-permute-start(f32[16,128]{1,0:T(8,128)S(1)} %merge.1.refs_4_.refs_0_), channel_id=1, source_target_pairs={{0,3},{1,2},{2,1},{3,0},{4,7},{5,6},{6,5},{7,4},{8,11},{9,10},{10,... | collective-permute-start | bytes 24584 | tf_op jit(solution)/shard_map/ppermute | solution.py:523
  17.6 2.3 %collective-permute-start.9 = (f32[16,128]{1,0:T(8,128)S(1)}, f32[16,128]{1,0:T(8,128)S(1)}, u32[]{:S(2)}, u32[]{:S(2)}) collective-permute-start(f32[16,128]{1,0:T(8,128)S(1)} %merge.1.refs_4_.refs_0_), channel_id=1, source_target_pairs={{0,1},{1,0},{2,3},{3,2},{4,5},{5,4},{6,7},{7,6},{8,9},{9,8},{10,11... | collective-permute-start | bytes 24584 | tf_op jit(solution)/shard_map/ppermute | solution.py:523
  18.1 1.8 %copy-start = (f32[3,384]{1,0:T(4,128)S(1)}, f32[3,384]{1,0:T(4,128)}, u32[]{:S(2)}) copy-start(f32[3,384]{1,0:T(4,128)} %refs_6_.3) | copy-start | bytes 13828
